TPU v7x, 128 devices: a whole 4x4x4 slice. The times are simulated.
128 devices in a mesh: row: 4 (over y), col: 32 (over x, z, core).
Axes of the slice: x: 4, y: 4, z: 4, core: 2. Of those that a mesh axis runs over, the one named last changes fastest.
Arguments:
- tokens: bfloat16 [16384, 1024], P(('row', 'col')), may hold values from -6 to 6
- lengths: int32 [128, 4], P(('row', 'col')), may hold values from 1 to 64, 128 in all within a row
- mixer_in: bfloat16 [1024, 4120], replicated, may hold values from -0.1875 to 0.1875
- conv_weight: float32 [4, 1792], replicated, may hold values from -3 to 3
- conv_bias: float32 [1792], replicated, may hold values from -3 to 3
- step_bias: float32 [24], replicated, may hold values from -3 to -1
- decay_log: float32 [24], replicated, may hold values from -4 to 2.5
- skip_gain: float32 [24], replicated, may hold values from 0.5 to 1.5
- ssm_gain: float32 [1536], replicated, may hold values from 0.5 to 1.5
- gain_in: float32 [1024], replicated, may hold values from 0.5 to 1.5
- mixer_out: bfloat16 [2048, 1024], replicated, may hold values from -0.1875 to 0.1875
- gain_mlp: float32 [1024], replicated, may hold values from 0.5 to 1.5
- w_gate: bfloat16 [1024, 2048], P('row', 'col'), may hold values from -0.1875 to 0.1875
- w_up: bfloat16 [1024, 2048], P('row', 'col'), may hold values from -0.1875 to 0.1875
- w_down: bfloat16 [2048, 1024], P('col', 'row'), may hold values from -0.125 to 0.125
- cotangent: bfloat16 [16384, 1024], P(('row', 'col')), may hold values from -6 to 6
Outputs:
- output: bfloat16 [16384, 1024], P(('row', 'col'))
- d_tokens: float32 [16384, 1024], P(('row', 'col'))
- grad_mixer_in: float32 [1024, 4120], P(('row', 'col'))
- grad_conv_weight: float32 [4, 1792], replicated
- grad_conv_bias: float32 [1792], replicated
- grad_step_bias: float32 [24], replicated
- grad_decay_log: float32 [24], replicated
- grad_skip_gain: float32 [24], replicated
- grad_ssm_gain: float32 [1536], replicated
- grad_gain_in: float32 [1024], replicated
- grad_mixer_out: float32 [2048, 1024], P(('row', 'col'))
- grad_gain_mlp: float32 [1024], replicated
- grad_w_gate: float32 [1024, 2048], P('row', 'col')
- grad_w_up: float32 [1024, 2048], P('row', 'col')
- grad_w_down: float32 [2048, 1024], P('col', 'row')
Inputs may be any that keep to these rules, and one draw needn't show every extreme that they name: Each row holds the lengths of the sequences on one device in order; they sum to 128, and the largest in each row is exactly 64.
All inputs are finite; a program needn't handle non-finite values.
Results may differ from a plain program's by a relative error of at most 0.018.
Values may be sent and summed in bfloat16 or wider, within the bound.
No kernel may reach another device: no remote copies, remote signals or barrier semaphores. Data moves between devices by JAX's collectives and lax.ppermute only.
A program may use at most 256 MiB of HBM per device.

v0:
```python
import math

import jax
import jax.numpy as jnp
from jax import lax
from jax.sharding import PartitionSpec as P

NH = 24
HEAD_SIZE = 64
NS = 128
QUERY_HEADS = 8
KEY_VALUE_HEADS = 2


norm_eps = 1e-05
rope_base = 100000000000.0


def turned_gather(arrays, axis, dims):
    turned = [jnp.moveaxis(a, dim, 0) for a, dim in zip(arrays, dims)]
    widths = [t[0].size for t in turned]
    both = jnp.concatenate([t.reshape(-1, w) for t, w in zip(turned, widths)], axis=1)
    out = lax.all_gather(both, axis, axis=0, tiled=True)
    pieces = jnp.split(out, [sum(widths[:k]) for k in range(1, len(widths))], axis=1)
    return tuple(
        (
            jnp.moveaxis(b.reshape(-1, *t.shape[1:]), 0, dim)
            for b, t, dim in zip(pieces, turned, dims)
        )
    )


def side_by_side(arrays, axis, dim, along):
    both = jnp.concatenate(arrays, axis=along)
    out, at, gathered = (lax.psum_scatter(both, axis, scatter_dimension=dim, tiled=True), 0, [])
    for a in arrays:
        gathered.append(lax.slice_in_dim(out, at, at + a.shape[along], axis=along))
        at += a.shape[along]
    return tuple(gathered)


def cut_along(array, dim, devices):
    shape = array.shape
    pieces = array.reshape(*shape[:dim], devices, shape[dim] // devices, *shape[dim + 1 :])
    return jnp.moveaxis(pieces, dim, 0)


def summed_on_arrival(array, axis, dim):
    devices = lax.axis_size(axis)
    pieces = lax.all_to_all(cut_along(array, dim, devices), axis, 0, 0, tiled=True)
    return jnp.sum(pieces.astype(jnp.float32), axis=0)


def side_by_side_2(arrays, axis, dim, along):
    widths = [a.shape[along] for a in arrays]
    both = jnp.concatenate(arrays, axis=along)
    out = summed_on_arrival(both, axis, dim)
    return tuple(jnp.split(out, [sum(widths[:k]) for k in range(1, len(widths))], axis=along))


def sum_together(arrays, axis, dims):
    devices = lax.axis_size(axis)
    pieces = [cut_along(a, dim, devices) for a, dim in zip(arrays, dims)]
    lines = jnp.concatenate([b.reshape(devices, -1) for b in pieces], axis=1)
    width = max(16, -(-lines.shape[1] // 1024) * 8)
    lines = jnp.pad(lines, ((0, 0), (0, width * 128 - lines.shape[1]))).reshape(-1, 128)
    ravelled, at, gathered = (lax.psum_scatter(lines, axis, tiled=True).reshape(-1), 0, [])
    for b in pieces:
        part = b[0]
        gathered.append(ravelled[at : at + part.size].reshape(part.shape))
        at += part.size
    return tuple(gathered)


def together(arrays, axis):
    ends = [0]
    for a in arrays:
        ends.append(ends[-1] + a.size)
    running = lax.psum(jnp.concatenate([a.ravel() for a in arrays]), axis)
    return tuple((running[b:e].reshape(a.shape) for a, b, e in zip(arrays, ends, ends[1:])))


def rms_norm(values, gain):
    return values * lax.rsqrt(jnp.mean(values * values, axis=-1, keepdims=True) + norm_eps) * gain


def layout(lens, token_count):
    ends = jnp.cumsum(lens)
    places = jnp.arange(token_count, dtype=jnp.int32)
    after = (places[:, None] >= ends[None, :]).astype(jnp.int32)
    segment = jnp.sum(after, axis=1)
    first = jnp.sum(after * lens[None, :], axis=1)
    return (segment, places - first)


def rotary_apply(values, cosine_table, sine_table):
    half = values.shape[-1] // 2
    front = values[..., :half]
    back = values[..., half:]
    return jnp.concatenate(
        [front * cosine_table - back * sine_table, back * cosine_table + front * sine_table],
        axis=-1,
    )


def mixer_core(
    projected, segment, position, conv_weight, conv_bias, step_bias, decay_log, skip_gain, ssm_gain
):
    token_count = projected.shape[0]
    inner = NH * HEAD_SIZE
    width = inner + 2 * NS
    places = jnp.arange(token_count, dtype=jnp.int32)
    out_gate = projected[:, :inner]
    conv_in = projected[:, inner : inner + width]
    step_in = projected[:, inner + width : inner + width + NH]
    attention_input = projected[:, inner + width + NH :]
    query_rows = attention_input[:, : QUERY_HEADS * HEAD_SIZE].reshape(
        token_count, QUERY_HEADS, HEAD_SIZE
    )
    every_key = attention_input[
        :, QUERY_HEADS * HEAD_SIZE : (QUERY_HEADS + KEY_VALUE_HEADS) * HEAD_SIZE
    ].reshape(token_count, KEY_VALUE_HEADS, HEAD_SIZE)
    every_value = attention_input[:, (QUERY_HEADS + KEY_VALUE_HEADS) * HEAD_SIZE :].reshape(
        token_count, KEY_VALUE_HEADS, HEAD_SIZE
    )
    taps = conv_weight.shape[0]
    summed = conv_bias + conv_weight[taps - 1] * conv_in
    for offset in range(1, taps):
        earlier = jnp.concatenate(
            [jnp.zeros((offset, width), jnp.float32), conv_in[: token_count - offset]], axis=0
        )
        prior_segment = jnp.concatenate(
            [jnp.full((offset,), -1, jnp.int32), segment[: token_count - offset]]
        )
        keep = (prior_segment == segment).astype(jnp.float32)[:, None]
        summed = summed + conv_weight[taps - 1 - offset] * earlier * keep
    active = jax.nn.silu(summed)
    heads_in = active[:, :inner].reshape(token_count, NH, HEAD_SIZE)
    state_in = active[:, inner : inner + NS]
    state_out = active[:, inner + NS :]
    delta = jax.nn.softplus(step_in + step_bias)
    running = jnp.cumsum(-delta * jnp.exp(decay_log), axis=0)
    allowed = (places[:, None] >= places[None, :]) & (segment[:, None] == segment[None, :])
    spread = running.T[:, :, None] - running.T[:, None, :]
    decay = jnp.where(allowed[None], jnp.exp(jnp.where(allowed[None], spread, 0.0)), 0.0)
    intersection = jnp.dot(state_out, state_in.T)
    mixing = intersection[None] * decay * delta.T[:, None, :]
    states = jnp.einsum("hts,shp->thp", mixing, heads_in) + skip_gain[None, :, None] * heads_in
    gated = states.reshape(token_count, inner) * jax.nn.silu(out_gate)
    ssm_out = rms_norm(gated, ssm_gain)
    half = HEAD_SIZE // 2
    frequency = rope_base ** (-jnp.arange(half, dtype=jnp.float32) / half)
    angles = position.astype(jnp.float32)[:, None] * frequency[None, :]
    cosine_table = jnp.cos(angles)[:, None, :]
    sine_table = jnp.sin(angles)[:, None, :]
    rotated_query = rotary_apply(query_rows, cosine_table, sine_table).reshape(
        token_count, KEY_VALUE_HEADS, QUERY_HEADS // KEY_VALUE_HEADS, HEAD_SIZE
    )
    turned_k = rotary_apply(every_key, cosine_table, sine_table)
    scores = jnp.einsum("tkgd,skd->kgts", rotated_query, turned_k) / math.sqrt(HEAD_SIZE)
    scores = jnp.where(allowed[None, None], scores, -1e30)
    attention_weights = jax.nn.softmax(scores, axis=-1)
    attended = jnp.einsum("kgts,skd->tkgd", attention_weights, every_value).reshape(
        token_count, QUERY_HEADS * HEAD_SIZE
    )
    return jnp.concatenate([ssm_out, attended], axis=1)


def contract_rows(left, right):
    return lax.dot_general(
        left, right, (((0,), (0,)), ((), ())), preferred_element_type=jnp.float32
    )


def contract_cols(left, right):
    return lax.dot_general(
        left, right, (((1,), (1,)), ((), ())), preferred_element_type=jnp.float32
    )


def gate_grads(d_hidden, gate, upper):
    sigma = jax.nn.sigmoid(gate)
    d_gate = d_hidden * upper * sigma * (1.0 + gate * (1.0 - sigma))
    d_upper = d_hidden * gate * sigma
    return jnp.concatenate([d_gate, d_upper], axis=1).astype(jnp.bfloat16)


def local(
    tokens,
    lengths,
    mixer_in,
    conv_weight,
    conv_bias,
    step_bias,
    decay_log,
    skip_gain,
    ssm_gain,
    gain_in,
    mixer_out,
    gain_mlp,
    w_gate,
    w_up,
    w_down,
    cotangent,
):
    token_count = tokens.shape[0]
    segment, position = layout(lengths[0], token_count)
    first_in = tokens.astype(jnp.float32)
    normed_first, first_pull = jax.vjp(rms_norm, first_in, gain_in)
    normed_first_low = normed_first.astype(jnp.bfloat16)
    projected = jnp.dot(normed_first_low, mixer_in, preferred_element_type=jnp.float32)

    def core_local(proj, kernel, kernel_bias, bias_step, log_decay, gain_skip, gain_ssm):
        return mixer_core(
            proj, segment, position, kernel, kernel_bias, bias_step, log_decay, gain_skip, gain_ssm
        )

    joined_wide, core_pull = jax.vjp(
        core_local, projected, conv_weight, conv_bias, step_bias, decay_log, skip_gain, ssm_gain
    )
    joined = joined_wide.astype(jnp.bfloat16)
    mixed = first_in + jnp.dot(joined, mixer_out, preferred_element_type=jnp.float32)
    normed_mlp, norm_pull = jax.vjp(rms_norm, mixed, gain_mlp)
    normed_low = normed_mlp.astype(jnp.bfloat16)
    rows_gate, rows_up, rows_down = turned_gather((w_gate, w_up, w_down), "row", (0, 0, 1))
    full_gate, full_up, full_down = turned_gather((rows_gate, rows_up, rows_down), "col", (1, 1, 0))
    hidden_units = full_gate.shape[1]
    w_pair = jnp.concatenate([full_gate, full_up], axis=1)
    gate_up = jnp.dot(normed_low, w_pair, preferred_element_type=jnp.float32)
    gate = gate_up[:, :hidden_units]
    upper = gate_up[:, hidden_units:]
    hidden = (jax.nn.silu(gate) * upper).astype(jnp.bfloat16)
    output = (mixed + jnp.dot(hidden, full_down, preferred_element_type=jnp.float32)).astype(
        jnp.bfloat16
    )
    d_hidden = contract_cols(cotangent, full_down)
    d_pair = gate_grads(d_hidden, gate, upper)
    whole_pair = contract_rows(normed_low, d_pair)
    whole_down = contract_rows(hidden, cotangent)
    d_normed = contract_cols(d_pair, w_pair)
    grad_gate, grad_up, grad_down = (
        *tuple(
            (
                part.astype(jnp.float32)
                for part in side_by_side(
                    (
                        whole_pair[:, :hidden_units].astype(jnp.bfloat16),
                        whole_pair[:, hidden_units:].astype(jnp.bfloat16),
                    ),
                    "col",
                    1,
                    0,
                )
            )
        ),
        lax.psum_scatter(
            whole_down.astype(jnp.bfloat16), "col", scatter_dimension=0, tiled=True
        ).astype(jnp.float32),
    )
    grad_gate, grad_up, grad_down = (
        *side_by_side_2(
            (grad_gate.astype(jnp.bfloat16), grad_up.astype(jnp.bfloat16)), "row", 0, 1
        ),
        summed_on_arrival(grad_down.astype(jnp.bfloat16), "row", 1),
    )
    d_mixed, d_gain_mlp = norm_pull(d_normed)
    d_mixed = d_mixed + cotangent.astype(jnp.float32)
    d_term = d_mixed.astype(jnp.bfloat16)
    local_out = contract_rows(joined, d_term)
    d_joined = contract_cols(d_term, mixer_out)
    core_grads = core_pull(d_joined)
    d_projected = core_grads[0].astype(jnp.bfloat16)
    local_in = contract_rows(normed_first_low, d_projected)
    d_normed_first = contract_cols(d_projected, mixer_in)
    d_first, d_gain_in = first_pull(d_normed_first)
    d_tokens = d_mixed + d_first
    grad_in, grad_out = sum_together((local_in, local_out), ("row", "col"), (0, 0))
    smalls = together(
        (
            core_grads[1],
            core_grads[2],
            core_grads[3],
            core_grads[4],
            core_grads[5],
            core_grads[6],
            d_gain_in,
            d_gain_mlp,
        ),
        ("row", "col"),
    )
    return (
        output,
        d_tokens,
        grad_in,
        smalls[0],
        smalls[1],
        smalls[2],
        smalls[3],
        smalls[4],
        smalls[5],
        smalls[6],
        grad_out,
        smalls[7],
        grad_gate,
        grad_up,
        grad_down,
    )


def solution(mesh):
    placed = (
        P(("row", "col"), None),
        P(("row", "col"), None),
        P(),
        P(),
        P(),
        P(),
        P(),
        P(),
        P(),
        P(),
        P(),
        P(),
        P("row", "col"),
        P("row", "col"),
        P("col", "row"),
        P(("row", "col"), None),
    )
    return jax.shard_map(
        local,
        mesh=mesh,
        in_specs=placed,
        out_specs=(
            P(("row", "col"), None),
            P(("row", "col"), None),
            P(("row", "col"), None),
            P(),
            P(),
            P(),
            P(),
            P(),
            P(),
            P(),
            P(("row", "col"), None),
            P(),
            P("row", "col"),
            P("row", "col"),
            P("col", "row"),
        ),
        check_vma=False,
    )
```

profile of v0, /device:TPU:0, one launch (start us, length us, event | category | flops | bytes accessed | tf_op | source)
XLA Modules:
  0.0 977.6 jit_solution(1523969317847147792)
XLA Ops:
  8.0 13.1 %all_gather.6 = bf16[1024,192]{0,1:T(8,128)(2,1)S(1)} all-gather(bf16[256,192]{0,1:T(8,128)(2,1)S(1)} %pad_maximum_fusion.13), channel_id=1, replica_groups=mesh['row'=4,'col'=32] {'row'}, dimensions={0}, use_global_device_ids=true | all-gather | bytes 491520 | tf_op jit(solution)/shard_map/all_gather | solution.py:23
  22.0 1.1 fusion.60
  23.7 5.0 fusion.79
  28.8 1.0 slice.168
  29.9 1.1 slice.166
  34.3 1.0 slice_reduce_fusion.3
  35.4 4.7 fusion.36
  44.0 1.6 multiply_reduce_fusion.13
  46.6 40.6 %all-gather.2.cloned.1.call-done = bf16[2048,3072]{1,0:T(8,128)(2,1)} async-done(((bf16[64,3072]{1,0:T(8,128)(2,1)}), bf16[2048,3072]{1,0:T(8,128)(2,1)}) %all-gather.2.cloned.1.call-update) | async-done | bytes 12582928 | tf_op jit(solution)/shard_map/all_gather | solution.py:23
  87.2 5.5 slice_bitcast_fusion.1
  92.7 7.2 fusion.1
  99.9 2.8 multiply_convert_fusion.1
  103.6 3.3 convolution_convert_fusion.1
  107.1 1.3 multiply_divide_fusion
  108.4 6.0 multiply_reduce_fusion.10
  114.6 1.5 fusion.72
  117.8 2.3 copy.96
  120.1 1.7 copy.76
  121.8 2.4 multiply_reduce_fusion.6
  124.8 3.9 multiply_reduce_fusion.7
  129.6 2.3 fusion.38
  132.0 1.1 reduce_window_sum.30
  133.8 3.7 convolution_convert_fusion
  137.5 4.0 fusion.117
  141.5 8.4 pad_maximum_fusion.1
  149.9 11.7 %copy.94 = bf16[2048,2048]{0,1:T(8,128)(2,1)} copy(bf16[2048,2048]{1,0:T(8,128)(2,1)} %pad_maximum_fusion.1) | data formatting | bytes 16777216
  162.6 4.5 fusion.70
  167.2 9.7 reshape_reshape.7
  177.0 1.4 multiply_reduce_fusion.11
  178.4 1.4 convolution_bitcast_fusion
  181.0 1.0 fusion.87
  182.0 1.1 fusion.83
  184.6 1.1 multiply_reduce_fusion.4
  189.2 8.5 fusion.77
  197.7 19.9 %reshape_reshape.6 = f32[128,32960]{1,0:T(8,128)} reshape(f32[1024,4120]{1,0:T(8,128)} %fusion.77) | data formatting | bytes 33751040 | tf_op jit(solution)/shard_map/reshape;reshape | solution.py:64
  217.6 20.5 %select_maximum_fusion = f32[128,50176]{1,0:T(8,128)} fusion(f32[128,16384]{1,0:T(8,128)} %reshape_reshape.7, f32[128,32960]{1,0:T(8,128)} %reshape_reshape.6), kind=kLoop, calls=%fused_computation | loop fusion | flops 25690112 | bytes 50954240 | tf_op jit(solution)/shard_map/concatenate | solution.py:64
  238.1 23.5 %reshape.417 = f32[50176,128]{1,0:T(8,128)} reshape(f32[128,50176]{1,0:T(8,128)} %select_maximum_fusion) | data formatting | bytes 51380224 | tf_op jit(solution)/shard_map/reshape | solution.py:66
  263.1 5.9 fusion.57
  269.1 66.9 %psum.7 = f32[12616]{0:T(1024)S(1)} all-reduce(f32[12616]{0:T(1024)S(1)} %concatenate.71), channel_id=1, replica_groups=mesh['row'=4,'col'=32] {'row','col'}, use_global_device_ids=true, to_apply=%region_31.32 | all-reduce | flops 12616 | bytes 100928 | tf_op jit(solution)/shard_map/psum | solution.py:79
  336.7 2.0 fusion.59
  338.8 3.9 fusion.31
  342.7 1.6 copy.101
  344.2 3.9 all-to-all-start.1
  348.2 1.0 fusion.118
  350.4 3.8 all-to-all-done.1
  354.1 3.4 all-to-all-start
  360.7 3.5 all-to-all-done
  365.8 601.6 %reduce-scatter.13.cloned.1.call-done = f32[392,128]{1,0:T(8,128)} async-done(((f32[50176,128]{1,0:T(8,128)}), f32[392,128]{1,0:T(8,128)}) %reduce-scatter.13.cloned.1.call-update) | async-done | bytes 200720
  (319 shorter events, 33.8 us)
Async XLA Ops:
  7.2 80.0 %all-gather.2.cloned.1.call-start = ((), (), s32[]{:S(2)}) async-start(), calls=%async_computation.5 | async-start | bytes 12976128 | tf_op jit(solution)/shard_map/all_gather | solution.py:23
  22.0 320.7 %reduce-scatter.9.cloned.1.call-start = ((), (), s32[]{:S(2)}) async-start(), calls=%async_computation.6 | async-start | bytes 4325376 | tf_op jit(solution)/shard_map/reduce_scatter | solution.py:256
  28.8 13.9 %copy-start.42 = (bf16[128,128]{0,1:T(8,128)(2,1)}, bf16[128,128]{0,1:T(8,128)(2,1)S(1)}, u32[]{:S(2)}) copy-start(bf16[128,128]{0,1:T(8,128)(2,1)S(1)} %slice.174) | copy-start | bytes 98308
  29.9 10.3 %copy-start.5 = (f32[126,1792]{0,1:T(8,128)}, f32[126,1792]{0,1:T(8,128)S(1)}, u32[]{:S(2)}) copy-start(f32[126,1792]{0,1:T(8,128)S(1)} %slice.167) | copy-start | bytes 2709508
  32.5 9.0 copy-start.57
  32.6 10.0 %copy-start.39 = (pred[128,128]{0,1:T(8,128)(4,1)}, pred[128,128]{0,1:T(8,128)(4,1)S(1)}, u32[]{:S(2)}) copy-start(pred[128,128]{0,1:T(8,128)(4,1)S(1)} %copy.73) | copy-start | bytes 49156
  33.6 6.6 copy-start.103
  35.2 5.6 copy-start.46
  35.2 5.6 copy-start.48
  35.3 5.6 copy-start.50
  35.3 5.6 copy-start.52
  35.4 5.1 copy-start.90
  35.4 6.1 copy-start.75
  35.4 6.1 copy-start.78
  35.4 6.1 copy-start.104
  46.6 46.1 %copy-start.44 = (f32[1024]{0:T(1024)S(1)}, f32[1024]{0:T(1024)}, u32[]{:S(2)}) copy-start(f32[1024]{0:T(1024)} %param.27) | copy-start | bytes 12292
  87.2 5.5 copy-start.14
  87.2 5.5 copy-start.82
  87.2 12.7 %slice-start = ((s8[12582912]{0:T(1024)(128)(4,1)}), s8[4194304]{0:T(1024)(128)(4,1)S(1)}, s32[]{:S(2)}) async-start(s8[12582912]{0:T(1024)(128)(4,1)} %bitcast.148), calls=%async_computation.9 | async-start | bytes 8388608
  87.2 12.7 %slice-start.1 = ((s8[12582912]{0:T(1024)(128)(4,1)}), s8[4194304]{0:T(1024)(128)(4,1)S(1)}, s32[]{:S(2)}) async-start(s8[12582912]{0:T(1024)(128)(4,1)} %bitcast.148), calls=%async_computation.10 | async-start | bytes 8388608
  92.7 7.2 copy-start.19
  92.7 7.2 slice-start.2
  92.7 7.2 copy-start.23
  106.9 241.3 %reduce-scatter.11.cloned.1.call-start = ((), (), s32[]{:S(2)}) async-start(), calls=%async_computation.7 | async-start | bytes 8650752
  108.4 6.0 copy-start.101
  108.4 6.0 copy-start.15
  108.4 6.0 copy-start.24
  108.4 6.0 copy-start.83
  108.4 6.2 copy-start.1
  121.8 7.8 copy-start.28
  121.8 7.8 copy-start.55
  121.8 7.8 copy-start.58
  121.8 7.8 copy-start.76
  121.8 7.8 copy-start.79
  161.6 805.8 %reduce-scatter.13.cloned.1.call-start = ((), (), s32[]{:S(2)}) async-start(), calls=%async_computation.8 | async-start | bytes 25890816
  167.2 9.8 %copy-start.31 = (bf16[128,512]{0,1:T(8,128)(2,1)S(1)}, bf16[128,512]{0,1:T(8,128)(2,1)}, u32[]{:S(2)}) copy-start(bf16[128,512]{0,1:T(8,128)(2,1)} %copy.76) | copy-start | bytes 393220
  167.2 9.8 %copy-start.40 = (pred[128,128]{0,1:T(8,128)(4,1)S(1)}, pred[128,128]{0,1:T(8,128)(4,1)}, u32[]{:S(2)}) copy-start(pred[128,128]{0,1:T(8,128)(4,1)} %copy-done.39) | copy-start | bytes 49156
  167.2 9.8 %copy-start.43 = (bf16[128,128]{0,1:T(8,128)(2,1)S(1)}, bf16[128,128]{0,1:T(8,128)(2,1)}, u32[]{:S(2)}) copy-start(bf16[128,128]{0,1:T(8,128)(2,1)} %copy-done.42) | copy-start | bytes 98308
  167.2 9.8 %copy-start.66 = (f32[2,4,128]{2,1,0:T(4,128)S(1)}, f32[2,4,128]{2,1,0:T(4,128)}, u32[]{:S(2)}) copy-start(f32[2,4,128]{2,1,0:T(4,128)} %copy-done.65) | copy-start | bytes 12292
  167.2 9.8 %copy-start.73 = (f32[2,4,128]{2,1,0:T(4,128)S(1)}, f32[2,4,128]{2,1,0:T(4,128)}, u32[]{:S(2)}) copy-start(f32[2,4,128]{2,1,0:T(4,128)} %multiply_divide_fusion) | copy-start | bytes 12292
  167.2 11.2 %copy-start.33 = (bf16[128,8,64]{0,2,1:T(8,128)(2,1)S(1)}, bf16[128,8,64]{0,2,1:T(8,128)(2,1)}, u32[]{:S(2)}) copy-start(bf16[128,8,64]{0,2,1:T(8,128)(2,1)} %copy-done.32) | copy-start | bytes 393220
  167.2 11.2 %copy-start.72 = (f32[2,4,128]{2,1,0:T(4,128)S(1)}, f32[2,4,128]{2,1,0:T(4,128)}, u32[]{:S(2)}) copy-start(f32[2,4,128]{2,1,0:T(4,128)} %copy-done.71) | copy-start | bytes 12292
  167.2 11.2 %copy-start.74 = (pred[128,128]{1,0:T(8,128)(4,1)S(1)}, pred[128,128]{1,0:T(8,128)(4,1)}, u32[]{:S(2)}) copy-start(pred[128,128]{1,0:T(8,128)(4,1)} %get-tuple-element.114) | copy-start | bytes 49156
  263.1 5.9 copy-start.68
  263.1 5.9 copy-start.92
  263.1 72.9 %copy-start.98 = (f32[128]{0:T(128)S(1)}, f32[128]{0:T(128)}, u32[]{:S(2)}) copy-start(f32[128]{0:T(128)} %copy-done.97) | copy-start | bytes 1540
  344.2 9.9 %all-to-all-start.1 = ((bf16[4,64,256]{2,1,0:T(8,128)(2,1)}), bf16[4,64,256]{2,1,0:T(8,128)(2,1)S(1)}, u32[]{:S(2)}, u32[]{:S(2)}) async-start(bf16[4,64,256]{2,1,0:T(8,128)(2,1)} %bitcast.143), calls=%async_computation.2 | async-start | bytes 262144 | tf_op jit(solution)/shard_map/all_to_all | solution.py:50
  354.1 10.1 %all-to-all-start = ((bf16[4,256,128]{2,1,0:T(8,128)(2,1)}), bf16[4,256,128]{2,1,0:T(8,128)(2,1)S(1)}, u32[]{:S(2)}, u32[]{:S(2)}) async-start(bf16[4,256,128]{2,1,0:T(8,128)(2,1)} %bitcast.57), calls=%async_computation | async-start | bytes 524288 | tf_op jit(solution)/shard_map/all_to_all | solution.py:50
  (69 other events, 160.0 us)
Sparse Core Ops, SparseCore 0:
  22.1 65.0 all-gather.1
  107.0 81.5 reduce-scatter.8
  192.8 92.0 reduce-scatter.10
  287.2 680.1 reduce-scatter.12
where the time goes:
time: 988 us; the launch traced here: 978 us
  waiting for transfers between devices  650 us (66%)
  local copies, waits for them, and re-layouts  103 us (10%)
  blocking collectives  80.1 us (8%)
  matrix products  63.6 us (6%)
  other arithmetic  57.9 us (6%)
  between operations  15.7 us (2%)
    unnamed x6, waiting for transfers between devices  602 us
    psum x1, blocking collectives, together(): running = lax.psum(jnp.concatenate([a.ravel() for a in arrays]), axis)  66.9 us
    all_gather x1, waiting for transfers between devices, turned_gather(): out = lax.all_gather(both, axis, axis=0, tiled=True)  40.6 us
    another operation x2, local copies, waits for them, and re-layouts, sum_together(): lines = jnp.concatenate([b.reshape(devices, -1) for b in pieces], axis=1)  29.6 us
    reshape x1, local copies, waits for them, and re-layouts, sum_together(): jnp.pad(lines, ((0, 0), (0, width * 128 - lines.shape[1]))).reshape(-1, 128)  23.5 us
    unnamed x228, local copies, waits for them, and re-layouts  23 us
    concatenate x1, other arithmetic, sum_together(): lines = jnp.concatenate([b.reshape(devices, -1) for b in pieces], axis=1)  20.5 us
    dot_general x4, matrix products, contract_rows(): lax.dot_general(left, right, (((0,), (0,)), ((), ())), preferred_element_...  20 us
  transfers between devices with their start and end apart: 6, of which 4 were waited for; matrix products, arithmetic and copies ran while one was open for 20% of the time, Pallas kernels for 0%

commit v1 on v0

v1 whole, which is shorter than its diff:
```python
import math

import jax
import jax.numpy as jnp
from jax import lax
from jax.experimental import pallas as pl
from jax.experimental.pallas import tpu as pltpu
from jax.sharding import Mesh, PartitionSpec as P

NH = 24
HEAD_SIZE = 64
NS = 128
QUERY_HEADS = 8
KEY_VALUE_HEADS = 2
INNER = NH * HEAD_SIZE
CONVW = INNER + 2 * NS
QKV = (QUERY_HEADS + 2 * KEY_VALUE_HEADS) * HEAD_SIZE

norm_eps = 1e-05
rope_base = 100000000000.0
f32 = jnp.float32
bf16 = jnp.bfloat16

ALL = ("y", "x", "z", "core")
CHIPS = ("y", "x", "z")
COL = ("x", "z", "core")
AXIS = 4


def moved(array, axis, shift):
    size = lax.axis_size(axis)
    return lax.ppermute(array, axis, [(i, (i + shift) % size) for i in range(size)])


def turned(array, axis, dim):
    twice = jnp.concatenate([array, array], axis=dim)
    return lax.dynamic_slice_in_dim(twice, lax.axis_index(axis), AXIS, axis=dim)


def added(first, others):
    total = first.astype(f32)
    for o in others:
        total = total + o.astype(f32)
    return total


def rms_norm(values, gain):
    return values * lax.rsqrt(jnp.mean(values * values, axis=-1, keepdims=True) + norm_eps) * gain


def layout(lens, token_count):
    ends = jnp.cumsum(lens)
    places = jnp.arange(token_count, dtype=jnp.int32)
    after = (places[:, None] >= ends[None, :]).astype(jnp.int32)
    segment = jnp.sum(after, axis=1)
    first = jnp.sum(after * lens[None, :], axis=1)
    return (segment, places - first)


def rotary_apply(values, cosine_table, sine_table):
    half = values.shape[-1] // 2
    front = values[..., :half]
    back = values[..., half:]
    return jnp.concatenate(
        [front * cosine_table - back * sine_table, back * cosine_table + front * sine_table],
        axis=-1,
    )


def mixer_core(
    out_gate,
    conv_in,
    step_in,
    attention_input,
    segment,
    position,
    conv_weight,
    conv_bias,
    step_bias,
    decay_log,
    skip_gain,
    ssm_gain,
):
    token_count = out_gate.shape[0]
    inner = INNER
    width = CONVW
    places = jnp.arange(token_count, dtype=jnp.int32)
    query_rows = attention_input[:, : QUERY_HEADS * HEAD_SIZE].reshape(
        token_count, QUERY_HEADS, HEAD_SIZE
    )
    every_key = attention_input[
        :, QUERY_HEADS * HEAD_SIZE : (QUERY_HEADS + KEY_VALUE_HEADS) * HEAD_SIZE
    ].reshape(token_count, KEY_VALUE_HEADS, HEAD_SIZE)
    every_value = attention_input[:, (QUERY_HEADS + KEY_VALUE_HEADS) * HEAD_SIZE :].reshape(
        token_count, KEY_VALUE_HEADS, HEAD_SIZE
    )
    taps = conv_weight.shape[0]
    summed = conv_bias + conv_weight[taps - 1] * conv_in
    for offset in range(1, taps):
        earlier = jnp.concatenate(
            [jnp.zeros((offset, width), jnp.float32), conv_in[: token_count - offset]], axis=0
        )
        prior_segment = jnp.concatenate(
            [jnp.full((offset,), -1, jnp.int32), segment[: token_count - offset]]
        )
        keep = (prior_segment == segment).astype(jnp.float32)[:, None]
        summed = summed + conv_weight[taps - 1 - offset] * earlier * keep
    active = jax.nn.silu(summed)
    heads_in = active[:, :inner].reshape(token_count, NH, HEAD_SIZE)
    state_in = active[:, inner : inner + NS]
    state_out = active[:, inner + NS :]
    delta = jax.nn.softplus(step_in + step_bias)
    running = jnp.cumsum(-delta * jnp.exp(decay_log), axis=0)
    allowed = (places[:, None] >= places[None, :]) & (segment[:, None] == segment[None, :])
    spread = running.T[:, :, None] - running.T[:, None, :]
    decay = jnp.where(allowed[None], jnp.exp(jnp.where(allowed[None], spread, 0.0)), 0.0)
    intersection = jnp.dot(state_out, state_in.T)
    mixing = intersection[None] * decay * delta.T[:, None, :]
    states = jnp.einsum("hts,shp->thp", mixing, heads_in) + skip_gain[None, :, None] * heads_in
    gated = states.reshape(token_count, inner) * jax.nn.silu(out_gate)
    ssm_out = rms_norm(gated, ssm_gain)
    half = HEAD_SIZE // 2
    frequency = rope_base ** (-jnp.arange(half, dtype=jnp.float32) / half)
    angles = position.astype(jnp.float32)[:, None] * frequency[None, :]
    cosine_table = jnp.cos(angles)[:, None, :]
    sine_table = jnp.sin(angles)[:, None, :]
    rotated_query = rotary_apply(query_rows, cosine_table, sine_table).reshape(
        token_count, KEY_VALUE_HEADS, QUERY_HEADS // KEY_VALUE_HEADS, HEAD_SIZE
    )
    turned_k = rotary_apply(every_key, cosine_table, sine_table)
    scores = jnp.einsum("tkgd,skd->kgts", rotated_query, turned_k) / math.sqrt(HEAD_SIZE)
    scores = jnp.where(allowed[None, None], scores, -1e30)
    attention_weights = jax.nn.softmax(scores, axis=-1)
    attended = jnp.einsum("kgts,skd->tkgd", attention_weights, every_value).reshape(
        token_count, QUERY_HEADS * HEAD_SIZE
    )
    return jnp.concatenate([ssm_out, attended], axis=1)


def dot_nn(left, right):
    return lax.dot_general(left, right, (((1,), (0,)), ((), ())), preferred_element_type=f32)


def dot_nt(left, right):
    return lax.dot_general(left, right, (((1,), (1,)), ((), ())), preferred_element_type=f32)


def dot_tn(left, right):
    return lax.dot_general(left, right, (((0,), (0,)), ((), ())), preferred_element_type=f32)


FF_BLOCK = 256


def ffn_body(x_ref, ct_ref, w_ref, out_ref, dn_ref, dw_ref):
    @pl.when(pl.program_id(0) == 0)
    def _():
        out_ref[...] = jnp.zeros_like(out_ref)
        dn_ref[...] = jnp.zeros_like(dn_ref)

    x = x_ref[...]
    ct = ct_ref[...]
    chunks = w_ref.shape[0]
    part = w_ref.shape[2] // 3
    gate, up, d_hidden = 0.0, 0.0, 0.0
    for c in range(chunks):
        cols = slice(c * part, (c + 1) * part)
        gate = gate + dot_nt(x[:, cols], w_ref[c, :, :part])
        up = up + dot_nt(x[:, cols], w_ref[c, :, part : 2 * part])
        d_hidden = d_hidden + dot_nt(ct[:, cols], w_ref[c, :, 2 * part :])
    sigma = jax.nn.sigmoid(gate)
    silu = gate * sigma
    hidden = (silu * up).astype(bf16)
    d_gate = (d_hidden * up * sigma * (1.0 + gate * (1.0 - sigma))).astype(bf16)
    d_up = (d_hidden * silu).astype(bf16)
    dw_gate = dot_tn(d_gate, x).astype(bf16)
    dw_up = dot_tn(d_up, x).astype(bf16)
    dw_down = dot_tn(hidden, ct).astype(bf16)
    for c in range(chunks):
        cols = slice(c * part, (c + 1) * part)
        out_ref[:, cols] += dot_nn(hidden, w_ref[c, :, 2 * part :])
        dn_ref[:, cols] += dot_nn(d_gate, w_ref[c, :, :part]) + dot_nn(
            d_up, w_ref[c, :, part : 2 * part]
        )
        at = 3 * c * part
        dw_ref[:, at : at + part] = dw_gate[:, cols]
        dw_ref[:, at + part : at + 2 * part] = dw_up[:, cols]
        dw_ref[:, at + 2 * part : at + 3 * part] = dw_down[:, cols]


def feed_forward(x, ct, weights):
    chunks, units, wide = weights.shape
    tokens, width = x.shape
    whole = pl.BlockSpec((tokens, width), lambda i: (0, 0))
    return pl.pallas_call(
        ffn_body,
        grid=(units // FF_BLOCK,),
        in_specs=[whole, whole, pl.BlockSpec((chunks, FF_BLOCK, wide), lambda i: (0, i, 0))],
        out_specs=[whole, whole, pl.BlockSpec((FF_BLOCK, chunks * wide), lambda i: (i, 0))],
        out_shape=[
            jax.ShapeDtypeStruct((tokens, width), f32),
            jax.ShapeDtypeStruct((tokens, width), f32),
            jax.ShapeDtypeStruct((units, chunks * wide), bf16),
        ],
        compiler_params=pltpu.CompilerParams(vmem_limit_bytes=48 * 1024 * 1024),
        cost_estimate=pl.CostEstimate(
            flops=18 * tokens * width * units,
            bytes_accessed=4 * chunks * units * wide,
            transcendentals=tokens * units,
        ),
        name="feed_forward",
    )(x, ct, weights)


SMALL_WIDE = 1920


def local(
    tokens,
    lengths,
    mixer_in,
    conv_weight,
    conv_bias,
    step_bias,
    decay_log,
    skip_gain,
    ssm_gain,
    gain_in,
    mixer_out,
    gain_mlp,
    w_gate,
    w_up,
    w_down,
    cotangent,
):
    token_count, width = tokens.shape
    core = lax.axis_index("core")

    own = jnp.concatenate([w_gate.T, w_up.T, w_down], axis=1)
    weights = lax.all_gather(own, ALL, tiled=True).reshape(AXIS, -1, own.shape[1])

    segment, position = layout(lengths[0], token_count)
    first_in = tokens.astype(f32)
    normed_first, first_pull = jax.vjp(rms_norm, first_in, gain_in)
    normed_first_low = normed_first.astype(bf16)
    projected = jnp.dot(normed_first_low, mixer_in, preferred_element_type=f32)

    def core_local(out_gate, conv_in, step_in, qkv, *params):
        return mixer_core(out_gate, conv_in, step_in, qkv, segment, position, *params)

    joined_wide, core_pull = jax.vjp(
        core_local,
        projected[:, :INNER],
        projected[:, INNER : INNER + CONVW],
        projected[:, INNER + CONVW : INNER + CONVW + NH],
        projected[:, INNER + CONVW + NH :],
        conv_weight,
        conv_bias,
        step_bias,
        decay_log,
        skip_gain,
        ssm_gain,
    )
    joined = joined_wide.astype(bf16)
    mixed = first_in + jnp.dot(joined, mixer_out, preferred_element_type=f32)
    normed_mlp, norm_pull = jax.vjp(rms_norm, mixed, gain_mlp)
    ffn_out, d_normed, d_weights = feed_forward(normed_mlp.astype(bf16), cotangent, weights)
    output = (mixed + ffn_out).astype(bf16)

    ff = lax.psum_scatter(d_weights, COL, scatter_dimension=0, tiled=True)
    ff = turned(ff.reshape(ff.shape[0], AXIS, -1).swapaxes(0, 1), "y", 0)
    ff = added(ff[0], [moved(ff[k], "y", k) for k in range(1, AXIS)])
    part = ff.shape[1] // 3

    d_mixed, d_gain_mlp = norm_pull(d_normed)
    d_mixed = d_mixed + cotangent.astype(f32)
    d_term = d_mixed.astype(bf16)

    by_place = joined.T.reshape(AXIS**3, 2, -1, token_count).swapaxes(0, 1)
    theirs = lax.dynamic_index_in_dim(by_place, 1 - core, 0, False)
    mine = lax.dynamic_index_in_dim(by_place, core, 0, False)
    got = moved(jnp.dot(theirs.reshape(-1, token_count), d_term, preferred_element_type=f32).astype(bf16), "core", 1)
    out_sum = added(jnp.dot(mine.reshape(-1, token_count), d_term, preferred_element_type=f32), [got])
    out_sum = out_sum.astype(bf16).reshape(AXIS**3, -1, width)
    out_parts = lax.all_to_all(out_sum, CHIPS, 0, 0, tiled=True)
    grad_out = jnp.sum(out_parts.astype(f32), axis=0)

    d_joined = dot_nt(d_term, mixer_out)
    d_gate, d_conv, d_step, d_qkv, *d_params = core_pull(d_joined)
    d_gate, d_conv, d_step, d_qkv = (a.astype(bf16) for a in (d_gate, d_conv, d_step, d_qkv))
    d_projected = jnp.concatenate([d_gate, d_conv, d_step, d_qkv], axis=1)
    d_normed_first = dot_nt(d_projected, mixer_in)
    d_first, d_gain_in = first_pull(d_normed_first)
    d_tokens = d_mixed + d_first

    lefts = normed_first_low.T.reshape(AXIS, AXIS, AXIS, 2, -1, token_count)
    for dim, axis in enumerate(CHIPS):
        lefts = turned(lefts, axis, dim)
    groups = []
    spare = SMALL_WIDE - CONVW - NH
    rights = (
        jnp.concatenate([d_gate, d_qkv], axis=1),
        jnp.concatenate([d_conv, jnp.pad(d_step, ((0, 0), (0, spare)))], axis=1),
    )
    smalls = [*d_params, d_gain_in, d_gain_mlp]
    small = jnp.concatenate([s.ravel() for s in smalls])
    small = jnp.pad(small, (0, 8 * SMALL_WIDE - small.size)).reshape(8, SMALL_WIDE)
    small = lax.optimization_barrier(small.astype(bf16))
    small = added(small, [moved(small, "core", 1)])
    sums = []
    for right, order in zip(rights, ((3, 1, 2, 0, 4, 5), (3, 2, 1, 0, 4, 5))):
        left = lefts.transpose(order)
        theirs = lax.dynamic_index_in_dim(left, 1 - core, 0, False)
        mine = lax.dynamic_index_in_dim(left, core, 0, False)
        rows = theirs.size // AXIS // token_count
        got = moved(
            jnp.dot(theirs.reshape(-1, token_count), right, preferred_element_type=f32).astype(bf16), "core", 1
        ).reshape(AXIS, rows, -1)
        sums.append(
            [
                added(jnp.dot(mine[k].reshape(rows, token_count), right, preferred_element_type=f32), [got[k]]).astype(bf16)
                for k in range(AXIS)
            ]
        )
    a, b = sums
    small = lax.optimization_barrier(small.astype(bf16))
    a_in = [moved(a[k], "x", k) for k in range(1, AXIS)]
    b_in = [moved(jnp.concatenate([b[k], small]), "z", k) for k in range(1, AXIS)]
    small = (small.astype(f32) + b_in[1][-8:].astype(f32)) + (b_in[0][-8:].astype(f32) + b_in[2][-8:].astype(f32))
    rows = a[0].shape[0] // AXIS
    a = [added(a[0][k * rows : (k + 1) * rows], [r[k * rows : (k + 1) * rows] for r in a_in]).astype(bf16) for k in range(AXIS)]
    b = [added(b[0][k * rows : (k + 1) * rows], [r[k * rows : (k + 1) * rows] for r in b_in]).astype(bf16) for k in range(AXIS)]
    small = lax.optimization_barrier(small.astype(bf16))
    a_in = [moved(a[k], "z", k) for k in range(1, AXIS)]
    b_in = [moved(jnp.concatenate([b[k], small]), "x", k) for k in range(1, AXIS)]
    small = (small.astype(f32) + b_in[1][-8:].astype(f32)) + (b_in[0][-8:].astype(f32) + b_in[2][-8:].astype(f32))
    small = lax.optimization_barrier(small.astype(bf16))
    rows = rows // AXIS
    both = []
    for k in range(AXIS):
        at = slice(k * rows, (k + 1) * rows)
        both.append(
            jnp.concatenate(
                [
                    added(a[0][at], [r[at] for r in a_in]).astype(bf16),
                    added(b[0][at], [r[at] for r in b_in]).astype(bf16),
                    small,
                ],
                axis=1,
            )
        )
    got = [moved(both[k], "y", k) for k in range(1, AXIS)]
    grad_in = added(both[0], got)
    at = grad_in.shape[1] - SMALL_WIDE
    small = (small.astype(f32) + got[1][:, at:].astype(f32)) + (got[0][:, at:].astype(f32) + got[2][:, at:].astype(f32))
    flat, at, totals = small.ravel(), 0, []
    for s in smalls:
        totals.append(flat[at : at + s.size].reshape(s.shape))
        at += s.size
    wide_a = INNER + QKV
    grad_in = jnp.concatenate(
        [grad_in[:, :INNER], grad_in[:, wide_a : wide_a + CONVW + NH], grad_in[:, INNER:wide_a]], axis=1
    )
    return (
        output,
        d_tokens,
        grad_in,
        *totals[:7],
        grad_out,
        totals[7],
        ff[:, :part].T,
        ff[:, part : 2 * part].T,
        ff[:, 2 * part :],
    )


def solution(mesh):
    fine = Mesh(mesh.devices.reshape(AXIS, AXIS, AXIS, 2), ALL)
    rows = P(ALL, None)
    placed = (
        rows,
        rows,
        *((P(),) * 10),
        P("y", COL),
        P("y", COL),
        P(COL, "y"),
        rows,
    )
    return jax.shard_map(
        local,
        mesh=fine,
        in_specs=placed,
        out_specs=(
            rows,
            rows,
            rows,
            *((P(),) * 7),
            rows,
            P(),
            P("y", COL),
            P("y", COL),
            P(COL, "y"),
        ),
        check_vma=False,
    )
```

time: 988 us -> 298 us (0.30)
  waiting for transfers between devices: 650 us -> 128 us
  blocking collectives: 80.1 us -> 0 us
  local copies, waits for them, and re-layouts: 103 us -> 24 us
  starting transfers between devices: 7.65 us -> 42.7 us
  other arithmetic: 57.9 us -> 28.5 us
  matrix products: 63.6 us -> 41.1 us
  Pallas kernels: 0 us -> 16.3 us
    unnamed x6 -> x2, waiting for transfers between devices: 602 us -> 0.03 us
    psum x1 -> x0, blocking collectives: 66.9 us -> none  [together(): running = lax.psum(jnp.concatenate([a.ravel() for a in arrays]), axis)]
    ppermute x0 -> x22, waiting for transfers between devices: none -> 59.7 us  [moved(): lax.ppermute(array, axis, [(i, (i + shift) % size) for i in range(size)])]
    ppermute x0 -> x22, starting transfers between devices: none -> 33.5 us  [moved(): lax.ppermute(array, axis, [(i, (i + shift) % size) for i in range(size)])]
    another operation x2 -> x1, local copies, waits for them, and re-layouts: 29.6 us -> 0.82 us  [sum_together(): lines = jnp.concatenate([b.reshape(devices, -1) for b in pieces], axis=1)]
    concatenate x5 -> x9, other arithmetic: 31.4 us -> 2.96 us  [the longest x1 1.44 us: local(): own = jnp.concatenate([w_gate.T, w_up.T, w_down], axis=1)]
    reshape x6 -> x4, local copies, waits for them, and re-layouts: 27.2 us -> 1.67 us  [the longest x1 1.02 us: local(): ff = turned(ff.reshape(ff.shape[0], AXIS, -1).swapaxes(0, 1), 'y', 0)]
    dot_general x12 -> x16, matrix products: 53.8 us -> 29.5 us  [the longest x8 11 us: local(): jnp.dot(mine[k].reshape(rows, token_count), right, preferred_element_type...]
  transfers between devices with their start and end apart: 6 -> 25, of which waited for: 4 -> 11; matrix products, arithmetic and copies ran while one was open for 20% -> 29% of each run, Pallas kernels for 0% -> 0%
where the time goes in v1:
time: 298 us; the launch traced here: 296 us
  waiting for transfers between devices  128 us (43%)
  starting transfers between devices  42.7 us (14%)
  matrix products  41.1 us (14%)
  other arithmetic  28.5 us (10%)
  local copies, waits for them, and re-layouts  24 us (8%)
  Pallas kernels  16.3 us (5%)
  between operations  15.9 us (5%)
    ppermute x22, waiting for transfers between devices, moved(): lax.ppermute(array, axis, [(i, (i + shift) % size) for i in range(size)])  59.7 us
    all_gather x1, waiting for transfers between devices, local(): lax.all_gather(own, ALL, tiled=True).reshape(AXIS, -1, own.shape[1])  52.4 us
    ppermute x22, starting transfers between devices, moved(): lax.ppermute(array, axis, [(i, (i + shift) % size) for i in range(size)])  33.5 us
    pallas_call x1, Pallas kernels, feed_forward(): pl.pallas_call(ffn_body, grid=(units // FF_BLOCK,), in_specs=[whole, whol...  16.3 us
    all_to_all x1, waiting for transfers between devices, local(): out_parts = lax.all_to_all(out_sum, CHIPS, 0, 0, tiled=True)  15.6 us
    dot_general x8, matrix products, local(): jnp.dot(mine[k].reshape(rows, token_count), right, preferred_element_type...  11 us
    all_to_all x1, starting transfers between devices, local(): out_parts = lax.all_to_all(out_sum, CHIPS, 0, 0, tiled=True)  9.11 us
    unnamed x203, local copies, waits for them, and re-layouts  8.43 us
  transfers between devices with their start and end apart: 25, of which 11 were waited for; matrix products, arithmetic and copies ran while one was open for 29% of the time, Pallas kernels for 0%

profile of v1, /device:TPU:0, one launch (start us, length us, event | category | flops | bytes accessed | tf_op | source)
XLA Modules:
  0.0 296.2 jit_solution(5951923681270010981)
XLA Ops:
  7.2 1.4 pad_maximum_fusion.13
  10.4 5.0 %fusion.77 = f32[128,4120]{0,1:T(8,128)S(1)} fusion(bf16[1024,4120]{0,1:T(8,128)(2,1)} %param.18, bf16[128,1024]{1,0:T(8,128)(2,1)} %param.16, f32[1024]{0:T(1024)} %param.25, f32[128]{0:T(128)S(1)} %fusion.92), kind=kOutput, calls=%fused_computation.175 | convolution fusion | flops 1080557568 | bytes 10813952 | tf_op jit(solution)/shard_map/dot_general | solution.py:246
  15.5 1.1 slice.545
  18.9 4.6 %fusion.30 = (f32[128,1792]{0,1:T(8,128)S(1)}, f32[128,1792]{0,1:T(8,128)}) fusion(f32[128]{0:T(128)S(1)} %get-tuple-element.126, f32[125,1792]{0,1:T(8,128)} %slice.546, f32[1792]{0:T(1024)S(1)} %get-tuple-element.35, f32[128]{0:T(128)S(1)} %get-tuple-element.127, f32[126,1792]{0,1:T(8,128)} %slice.545, f32[1792]{0:T(1024)S(1)} %get-tuple-element.36, ...), kind=kLoop, calls=%fused_computation.58 | loop fusion | flops 3440640 | bytes 5499392 | tf_op jit(solution)/shard_map/jvp(jit(silu))/mul | solution.py:108
  27.5 1.1 fusion.83
  30.5 1.5 convolution_convert_fusion.3
  35.0 52.4 %all-gather.2.cloned.1.call-done = bf16[8192,768]{1,0:T(8,128)(2,1)} async-done(((bf16[64,768]{1,0:T(8,128)(2,1)}), bf16[8192,768]{1,0:T(8,128)(2,1)}) %all-gather.2.cloned.1.call-update) | async-done | bytes 12582928 | tf_op jit(solution)/shard_map/all_gather | solution.py:240
  87.4 16.3 %feed_forward.1 = (f32[128,1024]{1,0:T(8,128)S(1)}, f32[128,1024]{1,0:T(8,128)S(1)}, bf16[2048,3072]{1,0:T(8,128)(2,1)}) custom-call(bf16[128,1024]{1,0:T(8,128)(2,1)S(1)} %multiply_convert_fusion.1.x_ref, bf16[128,1024]{1,0:T(8,128)(2,1)S(1)} %copy-done, bf16[4,2048,768]{2,1,0:T(8,128)(2,1)} %bitcast.235), custom_call_target="tpu_custom_call" | custom-call | flops 4831838208 | bytes 25165824 | tf_op jit(solution)/shard_map/feed_forward/pallas_call | solution.py:195
  105.4 3.7 %fusion.99 = f32[128,2048]{1,0:T(8,128)S(1)} fusion(bf16[2048,1024]{1,0:T(8,128)(2,1)} %param.26, f32[128,1024]{1,0:T(8,128)S(1)} %get-tuple-element.79), kind=kOutput, calls=%fused_computation.248 | convolution fusion | flops 537001984 | bytes 5767168 | tf_op jit(solution)/shard_map/dot_general | solution.py:145
  111.0 2.5 copy.116
  113.5 2.4 multiply_reduce_fusion.6
  116.0 3.6 %multiply_reduce_fusion.7 = (f32[1536]{0:T(1024)}, f32[128,1536]{0,1:T(8,128)S(1)}, bf16[128,1536]{0,1:T(8,128)(2,1)}) fusion(f32[128,1792]{0,1:T(8,128)S(1)} %copy-done.9, f32[128,4120]{0,1:T(8,128)S(1)} %copy-done.2, f32[128,1536]{0,1:T(8,128)S(1)} %get-tuple-element.51, f32[128]{0:T(128)S(1)} %multiply_multiply_fusion.1, f32[128]{0:T(128)S(1)} %copy-done.76, ...), kind=kLoop, calls=%fused_computation.73 | loop fusion | flops 3930624 | bytes 5125120 | tf_op jit(solution)/shard_map/transpose(jvp())/reduce_sum | solution.py:119
  119.6 1.2 split.40
  120.9 2.5 fusion.32
  138.7 2.6 fusion.52
  142.9 1.9 convolution_convert_fusion.1
  147.5 1.4 concatenate.109
  149.5 1.6 convolution_convert_fusion.2
  152.3 1.3 add_convert_fusion.7
  153.6 1.3 add_convert_fusion.5
  155.0 1.5 add_convert_fusion.6
  156.6 3.1 %collective-permute-start.10 = (bf16[136,1920]{1,0:T(8,128)(2,1)S(1)}, bf16[136,1920]{1,0:T(8,128)(2,1)S(1)}, u32[]{:S(2)}, u32[]{:S(2)}) collective-permute-start(bf16[136,1920]{1,0:T(8,128)(2,1)S(1)} %get-tuple-element.118), channel_id=1, source_target_pairs={{0,4},{2,6},{4,0},{6,2},{1,5},{3,7},{5,1},{7,3},{8,12},{10,14},{12... | collective-permute-start | bytes 1566728 | tf_op jit(solution)/shard_map/ppermute | solution.py:32
  161.7 1.3 add_convert_fusion.8
  163.1 1.4 add_convert_fusion.3
  164.5 1.2 collective-permute-start.1
  165.6 1.4 add_convert_fusion.2
  167.0 2.8 collective-permute-start.2
  169.8 14.3 %collective-permute-done.10 = bf16[136,1920]{1,0:T(8,128)(2,1)S(1)} collective-permute-done((bf16[136,1920]{1,0:T(8,128)(2,1)S(1)}, bf16[136,1920]{1,0:T(8,128)(2,1)S(1)}, u32[]{:S(2)}, u32[]{:S(2)}) %collective-permute-start.10) | collective-permute-done | bytes 522272 | tf_op jit(solution)/shard_map/ppermute | solution.py:32
  184.1 20.2 %collective-permute-done.11 = bf16[136,1920]{1,0:T(8,128)(2,1)S(1)} collective-permute-done((bf16[136,1920]{1,0:T(8,128)(2,1)S(1)}, bf16[136,1920]{1,0:T(8,128)(2,1)S(1)}, u32[]{:S(2)}, u32[]{:S(2)}) %collective-permute-start.11) | collective-permute-done | bytes 522272 | tf_op jit(solution)/shard_map/ppermute | solution.py:32
  204.6 1.2 collective-permute-start.12
  205.8 1.4 add_convert_fusion.1
  207.2 2.2 collective-permute-start.3
  209.4 1.4 collective-permute-start.13
  210.8 1.6 collective-permute-done.12
  213.0 1.4 add_convert_fusion.4
  214.4 1.7 collective-permute-done.13
  216.1 18.3 %collective-permute-done.14 = bf16[40,1920]{1,0:T(8,128)(2,1)S(1)} collective-permute-done((bf16[40,1920]{1,0:T(8,128)(2,1)S(1)}, bf16[40,1920]{1,0:T(8,128)(2,1)S(1)}, u32[]{:S(2)}, u32[]{:S(2)}) %collective-permute-start.14) | collective-permute-done | bytes 153632 | tf_op jit(solution)/shard_map/ppermute | solution.py:32
  234.9 4.3 %collective-permute-start.5 = (bf16[32,2304]{1,0:T(8,128)(2,1)S(1)}, bf16[32,2304]{1,0:T(8,128)(2,1)S(1)}, u32[]{:S(2)}, u32[]{:S(2)}) collective-permute-start(bf16[32,2304]{1,0:T(8,128)(2,1)S(1)} %get-tuple-element.57), channel_id=1, source_target_pairs={{0,4},{2,6},{4,0},{6,2},{1,5},{3,7},{5,1},{7,3},{8,12},{10,14},{12... | collective-permute-start | bytes 442376 | tf_op jit(solution)/shard_map/ppermute | solution.py:32
  239.2 2.5 collective-permute-start.6
  242.3 1.6 collective-permute-done.5
  245.6 2.9 collective-permute-start.16
  248.4 1.3 collective-permute-start.17
  249.7 2.0 add_convert_fusion
  251.7 9.1 %all-to-all-start = ((bf16[64,16,1024]{2,1,0:T(8,128)(2,1)}), bf16[64,16,1024]{2,1,0:T(8,128)(2,1)S(1)}, u32[]{:S(2)}, u32[]{:S(2)}) async-start(bf16[64,16,1024]{2,1,0:T(8,128)(2,1)} %bitcast.181), calls=%async_computation | async-start | bytes 4194304 | tf_op jit(solution)/shard_map/all_to_all | solution.py:285
  266.1 1.6 collective-permute-start.19
  267.8 2.9 collective-permute-start.20
  270.7 1.4 collective-permute-start.21
  272.0 15.6 %all-to-all-done = bf16[64,16,1024]{2,1,0:T(8,128)(2,1)S(1)} async-done(((bf16[64,16,1024]{2,1,0:T(8,128)(2,1)}), bf16[64,16,1024]{2,1,0:T(8,128)(2,1)S(1)}, u32[]{:S(2)}, u32[]{:S(2)}) %all-to-all-start) | async-done | bytes 2097184 | tf_op jit(solution)/shard_map/all_to_all | solution.py:285
  (359 shorter events, 49.3 us)
Async XLA Ops:
  7.2 80.2 %all-gather.2.cloned.1.call-start = ((), (), s32[]{:S(2)}) async-start(), calls=%async_computation.2 | async-start | bytes 12681216 | tf_op jit(solution)/shard_map/all_gather | solution.py:240
  8.7 256.2 %reduce-scatter.2.cloned.1.call-start = ((), (), s32[]{:S(2)}) async-start(), calls=%async_computation.3 | async-start | bytes 12976128 | tf_op jit(solution)/shard_map/reduce_scatter | solution.py:270
  10.4 5.0 %copy-start.83 = (f32[128]{0:T(128)}, f32[128]{0:T(128)S(1)}, u32[]{:S(2)}) copy-start(f32[128]{0:T(128)S(1)} %fusion.92) | copy-start | bytes 1540
  15.4 14.6 %copy-start.1 = (f32[128,4120]{0,1:T(8,128)}, f32[128,4120]{0,1:T(8,128)S(1)}, u32[]{:S(2)}) copy-start(f32[128,4120]{0,1:T(8,128)S(1)} %fusion.77) | copy-start | bytes 6328324
  18.7 4.8 %copy-start.40 = (f32[1792]{0:T(1024)}, f32[1792]{0:T(1024)S(1)}, u32[]{:S(2)}) copy-start(f32[1792]{0:T(1024)S(1)} %get-tuple-element.33) | copy-start | bytes 21508
  18.7 4.8 %copy-start.42 = (f32[1792]{0:T(1024)}, f32[1792]{0:T(1024)S(1)}, u32[]{:S(2)}) copy-start(f32[1792]{0:T(1024)S(1)} %get-tuple-element.35) | copy-start | bytes 21508
  18.7 4.8 %copy-start.44 = (f32[1792]{0:T(1024)}, f32[1792]{0:T(1024)S(1)}, u32[]{:S(2)}) copy-start(f32[1792]{0:T(1024)S(1)} %get-tuple-element.34) | copy-start | bytes 21508
  18.7 4.8 %copy-start.46 = (f32[1792]{0:T(1024)}, f32[1792]{0:T(1024)S(1)}, u32[]{:S(2)}) copy-start(f32[1792]{0:T(1024)S(1)} %get-tuple-element.36) | copy-start | bytes 21508
  18.8 4.7 %copy-start.77 = (f32[128]{0:T(128)}, f32[128]{0:T(128)S(1)}, u32[]{:S(2)}) copy-start(f32[128]{0:T(128)S(1)} %get-tuple-element.125) | copy-start | bytes 1540
  18.8 4.7 %copy-start.79 = (f32[128]{0:T(128)}, f32[128]{0:T(128)S(1)}, u32[]{:S(2)}) copy-start(f32[128]{0:T(128)S(1)} %get-tuple-element.127) | copy-start | bytes 1540
  18.8 4.7 %copy-start.81 = (f32[128]{0:T(128)}, f32[128]{0:T(128)S(1)}, u32[]{:S(2)}) copy-start(f32[128]{0:T(128)S(1)} %get-tuple-element.126) | copy-start | bytes 1540
  27.5 6.0 %copy-start.62 = (f32[2,4,128]{2,1,0:T(4,128)}, f32[2,4,128]{2,1,0:T(4,128)S(1)}, u32[]{:S(2)}) copy-start(f32[2,4,128]{2,1,0:T(4,128)S(1)} %fusion.66) | copy-start | bytes 12292
  33.5 53.9 %copy-start = (bf16[128,1024]{1,0:T(8,128)(2,1)S(1)}, bf16[128,1024]{1,0:T(8,128)(2,1)}, u32[]{:S(2)}) copy-start(bf16[128,1024]{1,0:T(8,128)(2,1)} %ct_ref.1) | copy-start | bytes 786436
  111.0 4.9 %copy-start.2 = (f32[128,4120]{0,1:T(8,128)S(1)}, f32[128,4120]{0,1:T(8,128)}, u32[]{:S(2)}) copy-start(f32[128,4120]{0,1:T(8,128)} %copy-done.1) | copy-start | bytes 6328324
  116.0 4.8 %copy-start.23 = (f32[128,1536]{0,1:T(8,128)S(1)}, f32[128,1536]{0,1:T(8,128)}, u32[]{:S(2)}) copy-start(f32[128,1536]{0,1:T(8,128)} %slice.547) | copy-start | bytes 2359300
  116.0 4.8 %copy-start.49 = (f32[128,128]{1,0:T(8,128)S(1)}, f32[128,128]{1,0:T(8,128)}, u32[]{:S(2)}) copy-start(f32[128,128]{1,0:T(8,128)} %copy-done.48) | copy-start | bytes 196612
  116.0 4.8 %copy-start.52 = (pred[128,128]{1,0:T(8,128)(4,1)S(1)}, pred[128,128]{1,0:T(8,128)(4,1)}, u32[]{:S(2)}) copy-start(pred[128,128]{1,0:T(8,128)(4,1)} %copy-done.51) | copy-start | bytes 49156
  116.0 4.8 %copy-start.67 = (f32[24,128]{1,0:T(8,128)S(1)}, f32[24,128]{1,0:T(8,128)}, u32[]{:S(2)}) copy-start(f32[24,128]{1,0:T(8,128)} %copy-done.66) | copy-start | bytes 36868
  116.0 4.8 %copy-start.70 = (f32[24,128]{1,0:T(8,128)S(1)}, f32[24,128]{1,0:T(8,128)}, u32[]{:S(2)}) copy-start(f32[24,128]{1,0:T(8,128)} %copy-done.69) | copy-start | bytes 36868
  128.8 9.6 %copy-start.24 = (bf16[128,768]{0,1:T(8,128)(2,1)}, bf16[128,768]{0,1:T(8,128)(2,1)S(1)}, u32[]{:S(2)}) copy-start(bf16[128,768]{0,1:T(8,128)(2,1)S(1)} %add_convert_fusion.11) | copy-start | bytes 589828
  132.2 6.3 %slice-start = ((s8[8437760]{0:T(1024)(128)(4,1)}), s8[4194304]{0:T(1024)(128)(4,1)S(1)}, s32[]{:S(2)}) async-start(s8[8437760]{0:T(1024)(128)(4,1)} %bitcast.179), calls=%async_computation.4 | async-start | bytes 8388608
  132.9 5.6 %slice-start.1 = ((s8[8437760]{0:T(1024)(128)(4,1)}), s8[4194304]{0:T(1024)(128)(4,1)S(1)}, s32[]{:S(2)}) async-start(s8[8437760]{0:T(1024)(128)(4,1)} %bitcast.179), calls=%async_computation.5 | async-start | bytes 8388608
  144.9 7.4 %collective-permute-start.7 = (bf16[512,1920]{1,0:T(8,128)(2,1)}, bf16[512,1920]{1,0:T(8,128)(2,1)}, u32[]{:S(2)}, u32[]{:S(2)}) collective-permute-start(bf16[512,1920]{1,0:T(8,128)(2,1)} %convolution_convert_fusion.1), channel_id=1, source_target_pairs={{0,1},{1,0},{2,3},{3,2},{4,5},{5,4},{6,7},{7,6},{8,9},{9,8},{10,11... | collective-permute-start | bytes 5898248 | tf_op jit(solution)/shard_map/ppermute | solution.py:32
  146.8 16.3 %collective-permute-start = (bf16[512,2304]{1,0:T(8,128)(2,1)S(1)}, bf16[512,2304]{1,0:T(8,128)(2,1)}, u32[]{:S(2)}, u32[]{:S(2)}) collective-permute-start(bf16[512,2304]{1,0:T(8,128)(2,1)S(1)} %convolution_convert_fusion), channel_id=1, source_target_pairs={{0,1},{1,0},{2,3},{3,2},{4,5},{5,4},{6,7},{7,6},{8,9},{9,8},{10,11... | collective-permute-start | bytes 7077896 | tf_op jit(solution)/shard_map/ppermute | solution.py:32
  149.0 3.2 %collective-permute-start.8 = (bf16[8,1920]{1,0:T(8,128)(2,1)S(1)}, bf16[8,1920]{1,0:T(8,128)(2,1)S(1)}, u32[]{:S(2)}, u32[]{:S(2)}) collective-permute-start(bf16[8,1920]{1,0:T(8,128)(2,1)S(1)} %convert_element_type.501), channel_id=1, source_target_pairs={{0,1},{1,0},{2,3},{3,2},{4,5},{5,4},{6,7},{7,6},{8,9},{9,8},{10,11... | collective-permute-start | bytes 92168 | tf_op jit(solution)/shard_map/ppermute | solution.py:32
  156.6 6.5 %copy-start.20 = (bf16[128,1536]{0,1:T(8,128)(2,1)S(1)}, bf16[128,1536]{0,1:T(8,128)(2,1)}, u32[]{:S(2)}) copy-start(bf16[128,1536]{0,1:T(8,128)(2,1)} %get-tuple-element.54) | copy-start | bytes 1179652
  156.6 6.5 %copy-start.26 = (bf16[128,768]{0,1:T(8,128)(2,1)S(1)}, bf16[128,768]{0,1:T(8,128)(2,1)}, u32[]{:S(2)}) copy-start(bf16[128,768]{0,1:T(8,128)(2,1)} %copy-done.24) | copy-start | bytes 589828
  156.6 27.5 %collective-permute-start.10 = (bf16[136,1920]{1,0:T(8,128)(2,1)S(1)}, bf16[136,1920]{1,0:T(8,128)(2,1)S(1)}, u32[]{:S(2)}, u32[]{:S(2)}) collective-permute-start(bf16[136,1920]{1,0:T(8,128)(2,1)S(1)} %get-tuple-element.118), channel_id=1, source_target_pairs={{0,4},{2,6},{4,0},{6,2},{1,5},{3,7},{5,1},{7,3},{8,12},{10,14},{12... | collective-permute-start | bytes 1566728 | tf_op jit(solution)/shard_map/ppermute | solution.py:32
  159.7 44.6 %collective-permute-start.11 = (bf16[136,1920]{1,0:T(8,128)(2,1)S(1)}, bf16[136,1920]{1,0:T(8,128)(2,1)S(1)}, u32[]{:S(2)}, u32[]{:S(2)}) collective-permute-start(bf16[136,1920]{1,0:T(8,128)(2,1)S(1)} %get-tuple-element.119), channel_id=1, source_target_pairs={{0,6},{2,0},{4,2},{6,4},{1,7},{3,1},{5,3},{7,5},{8,14},{10,8},{12,... | collective-permute-start | bytes 1566728 | tf_op jit(solution)/shard_map/ppermute | solution.py:32
  160.7 43.5 %collective-permute-start.9 = (bf16[136,1920]{1,0:T(8,128)(2,1)S(1)}, bf16[136,1920]{1,0:T(8,128)(2,1)S(1)}, u32[]{:S(2)}, u32[]{:S(2)}) collective-permute-start(bf16[136,1920]{1,0:T(8,128)(2,1)S(1)} %get-tuple-element.120), channel_id=1, source_target_pairs={{0,2},{2,4},{4,6},{6,0},{1,3},{3,5},{5,7},{7,1},{8,10},{10,12},{12... | collective-permute-start | bytes 1566728 | tf_op jit(solution)/shard_map/ppermute | solution.py:32
  164.5 70.0 %collective-permute-start.1 = (bf16[128,2304]{1,0:T(8,128)(2,1)S(1)}, bf16[128,2304]{1,0:T(8,128)(2,1)S(1)}, u32[]{:S(2)}, u32[]{:S(2)}) collective-permute-start(bf16[128,2304]{1,0:T(8,128)(2,1)S(1)} %add_convert_fusion.3), channel_id=1, source_target_pairs={{0,8},{8,16},{16,24},{24,0},{1,9},{9,17},{17,25},{25,1},{2,10},{10... | collective-permute-start | bytes 1769480 | tf_op jit(solution)/shard_map/ppermute | solution.py:32
  167.0 67.5 %collective-permute-start.2 = (bf16[128,2304]{1,0:T(8,128)(2,1)S(1)}, bf16[128,2304]{1,0:T(8,128)(2,1)S(1)}, u32[]{:S(2)}, u32[]{:S(2)}) collective-permute-start(bf16[128,2304]{1,0:T(8,128)(2,1)S(1)} %add_convert_fusion.2), channel_id=1, source_target_pairs={{0,16},{8,24},{16,0},{24,8},{1,17},{9,25},{17,1},{25,9},{2,18},{10... | collective-permute-start | bytes 1769480 | tf_op jit(solution)/shard_map/ppermute | solution.py:32
  204.6 7.7 %collective-permute-start.12 = (bf16[40,1920]{1,0:T(8,128)(2,1)S(1)}, bf16[40,1920]{1,0:T(8,128)(2,1)S(1)}, u32[]{:S(2)}, u32[]{:S(2)}) collective-permute-start(bf16[40,1920]{1,0:T(8,128)(2,1)S(1)} %get-tuple-element.117), channel_id=1, source_target_pairs={{0,8},{8,16},{16,24},{24,0},{1,9},{9,17},{17,25},{25,1},{2,10},{10... | collective-permute-start | bytes 460808 | tf_op jit(solution)/shard_map/ppermute | solution.py:32
  207.2 27.3 %collective-permute-start.3 = (bf16[128,2304]{1,0:T(8,128)(2,1)S(1)}, bf16[128,2304]{1,0:T(8,128)(2,1)S(1)}, u32[]{:S(2)}, u32[]{:S(2)}) collective-permute-start(bf16[128,2304]{1,0:T(8,128)(2,1)S(1)} %add_convert_fusion.1), channel_id=1, source_target_pairs={{0,24},{8,0},{16,8},{24,16},{1,25},{9,1},{17,9},{25,17},{2,26},{10... | collective-permute-start | bytes 1769480 | tf_op jit(solution)/shard_map/ppermute | solution.py:32
  209.4 6.7 %collective-permute-start.13 = (bf16[40,1920]{1,0:T(8,128)(2,1)S(1)}, bf16[40,1920]{1,0:T(8,128)(2,1)S(1)}, u32[]{:S(2)}, u32[]{:S(2)}) collective-permute-start(bf16[40,1920]{1,0:T(8,128)(2,1)S(1)} %get-tuple-element.115), channel_id=1, source_target_pairs={{0,16},{8,24},{16,0},{24,8},{1,17},{9,25},{17,1},{25,9},{2,18},{10... | collective-permute-start | bytes 460808 | tf_op jit(solution)/shard_map/ppermute | solution.py:32
  212.3 22.1 %collective-permute-start.14 = (bf16[40,1920]{1,0:T(8,128)(2,1)S(1)}, bf16[40,1920]{1,0:T(8,128)(2,1)S(1)}, u32[]{:S(2)}, u32[]{:S(2)}) collective-permute-start(bf16[40,1920]{1,0:T(8,128)(2,1)S(1)} %get-tuple-element.116), channel_id=1, source_target_pairs={{0,24},{8,0},{16,8},{24,16},{1,25},{9,1},{17,9},{25,17},{2,26},{10... | collective-permute-start | bytes 460808 | tf_op jit(solution)/shard_map/ppermute | solution.py:32
  216.1 33.6 %collective-permute-start.18 = (bf16[1024,1024]{1,0:T(8,128)(2,1)S(1)}, bf16[1024,1024]{1,0:T(8,128)(2,1)S(1)}, u32[]{:S(2)}, u32[]{:S(2)}) collective-permute-start(bf16[1024,1024]{1,0:T(8,128)(2,1)S(1)} %convolution_convert_fusion.2), channel_id=1, source_target_pairs={{0,1},{1,0},{2,3},{3,2},{4,5},{5,4},{6,7},{7,6},{8,9},{9,8},{10,11... | collective-permute-start | bytes 6291464 | tf_op jit(solution)/shard_map/ppermute | solution.py:32
  234.5 15.2 %copy-start.21 = (bf16[64,1,16,128]{3,2,1,0:T(8,128)(2,1)S(1)}, bf16[64,1,16,128]{3,2,1,0:T(8,128)(2,1)}, u32[]{:S(2)}) copy-start(bf16[64,1,16,128]{3,2,1,0:T(8,128)(2,1)} %get-tuple-element.77) | copy-start | bytes 786436
  234.9 7.5 %collective-permute-start.4 = (bf16[32,2304]{1,0:T(8,128)(2,1)S(1)}, bf16[32,2304]{1,0:T(8,128)(2,1)S(1)}, u32[]{:S(2)}, u32[]{:S(2)}) collective-permute-start(bf16[32,2304]{1,0:T(8,128)(2,1)S(1)} %get-tuple-element.58), channel_id=1, source_target_pairs={{0,2},{2,4},{4,6},{6,0},{1,3},{3,5},{5,7},{7,1},{8,10},{10,12},{12... | collective-permute-start | bytes 442376 | tf_op jit(solution)/shard_map/ppermute | solution.py:32
  234.9 9.0 %collective-permute-start.5 = (bf16[32,2304]{1,0:T(8,128)(2,1)S(1)}, bf16[32,2304]{1,0:T(8,128)(2,1)S(1)}, u32[]{:S(2)}, u32[]{:S(2)}) collective-permute-start(bf16[32,2304]{1,0:T(8,128)(2,1)S(1)} %get-tuple-element.57), channel_id=1, source_target_pairs={{0,4},{2,6},{4,0},{6,2},{1,5},{3,7},{5,1},{7,3},{8,12},{10,14},{12... | collective-permute-start | bytes 442376 | tf_op jit(solution)/shard_map/ppermute | solution.py:32
  239.2 5.2 %collective-permute-start.6 = (bf16[32,2304]{1,0:T(8,128)(2,1)S(1)}, bf16[32,2304]{1,0:T(8,128)(2,1)S(1)}, u32[]{:S(2)}, u32[]{:S(2)}) collective-permute-start(bf16[32,2304]{1,0:T(8,128)(2,1)S(1)} %get-tuple-element.56), channel_id=1, source_target_pairs={{0,6},{2,0},{4,2},{6,4},{1,7},{3,1},{5,3},{7,5},{8,14},{10,8},{12,... | collective-permute-start | bytes 442376 | tf_op jit(solution)/shard_map/ppermute | solution.py:32
  244.5 16.3 %collective-permute-start.15 = (bf16[8,6144]{1,0:T(8,128)(2,1)S(1)}, bf16[8,6144]{1,0:T(8,128)(2,1)S(1)}, u32[]{:S(2)}, u32[]{:S(2)}) collective-permute-start(bf16[8,6144]{1,0:T(8,128)(2,1)S(1)} %get-tuple-element.112), channel_id=1, source_target_pairs={{0,32},{32,64},{64,96},{96,0},{1,33},{33,65},{65,97},{97,1},{2,34}... | collective-permute-start | bytes 294920 | tf_op jit(solution)/shard_map/ppermute | solution.py:32
  245.6 15.3 %collective-permute-start.16 = (bf16[8,6144]{1,0:T(8,128)(2,1)S(1)}, bf16[8,6144]{1,0:T(8,128)(2,1)S(1)}, u32[]{:S(2)}, u32[]{:S(2)}) collective-permute-start(bf16[8,6144]{1,0:T(8,128)(2,1)S(1)} %get-tuple-element.113), channel_id=1, source_target_pairs={{0,64},{32,96},{64,0},{96,32},{1,65},{33,97},{65,1},{97,33},{2,66}... | collective-permute-start | bytes 294920 | tf_op jit(solution)/shard_map/ppermute | solution.py:32
  248.4 12.4 %collective-permute-start.17 = (bf16[8,6144]{1,0:T(8,128)(2,1)S(1)}, bf16[8,6144]{1,0:T(8,128)(2,1)S(1)}, u32[]{:S(2)}, u32[]{:S(2)}) collective-permute-start(bf16[8,6144]{1,0:T(8,128)(2,1)S(1)} %get-tuple-element.114), channel_id=1, source_target_pairs={{0,96},{32,0},{64,32},{96,64},{1,97},{33,1},{65,33},{97,65},{2,98}... | collective-permute-start | bytes 294920 | tf_op jit(solution)/shard_map/ppermute | solution.py:32
  251.7 35.9 %all-to-all-start = ((bf16[64,16,1024]{2,1,0:T(8,128)(2,1)}), bf16[64,16,1024]{2,1,0:T(8,128)(2,1)S(1)}, u32[]{:S(2)}, u32[]{:S(2)}) async-start(bf16[64,16,1024]{2,1,0:T(8,128)(2,1)} %bitcast.181), calls=%async_computation | async-start | bytes 4194304 | tf_op jit(solution)/shard_map/all_to_all | solution.py:285
  266.1 22.5 %collective-permute-start.19 = (bf16[64,768]{1,0:T(8,128)(2,1)S(1)}, bf16[64,768]{1,0:T(8,128)(2,1)S(1)}, u32[]{:S(2)}, u32[]{:S(2)}) collective-permute-start(bf16[64,768]{1,0:T(8,128)(2,1)S(1)} %get-tuple-element.81), channel_id=1, source_target_pairs={{0,32},{32,64},{64,96},{96,0},{1,33},{33,65},{65,97},{97,1},{2,34}... | collective-permute-start | bytes 294920 | tf_op jit(solution)/shard_map/ppermute | solution.py:32
  267.8 20.9 %collective-permute-start.20 = (bf16[64,768]{1,0:T(8,128)(2,1)S(1)}, bf16[64,768]{1,0:T(8,128)(2,1)S(1)}, u32[]{:S(2)}, u32[]{:S(2)}) collective-permute-start(bf16[64,768]{1,0:T(8,128)(2,1)S(1)} %get-tuple-element.82), channel_id=1, source_target_pairs={{0,64},{32,96},{64,0},{96,32},{1,65},{33,97},{65,1},{97,33},{2,66}... | collective-permute-start | bytes 294920 | tf_op jit(solution)/shard_map/ppermute | solution.py:32
  270.7 18.0 %collective-permute-start.21 = (bf16[64,768]{1,0:T(8,128)(2,1)S(1)}, bf16[64,768]{1,0:T(8,128)(2,1)S(1)}, u32[]{:S(2)}, u32[]{:S(2)}) collective-permute-start(bf16[64,768]{1,0:T(8,128)(2,1)S(1)} %get-tuple-element.83), channel_id=1, source_target_pairs={{0,96},{32,0},{64,32},{96,64},{1,97},{33,1},{65,33},{97,65},{2,98}... | collective-permute-start | bytes 294920 | tf_op jit(solution)/shard_map/ppermute | solution.py:32
  (78 other events, 152.3 us)
Sparse Core Ops, SparseCore 0:
  11.6 75.7 all-gather.1
  103.9 133.0 reduce-scatter.1
